TPU v7x, 256 devices: a whole 4x4x8 slice. The times are simulated.
256 devices in a mesh: seq: 32 (over y, z), head: 8 (over x, core).
Axes of the slice: x: 4, y: 4, z: 8, core: 2. Of those that a mesh axis runs over, the one named last changes fastest.
Arguments:
- queries: bfloat16 [32768, 32, 128], P('seq', 'head'), may hold values from -6 to 6
- key_rows: bfloat16 [32768, 32, 128], P('seq', 'head'), may hold values from -6 to 6
- value_rows: bfloat16 [32768, 32, 128], P('seq', 'head'), may hold values from -6 to 6
- out_grad: bfloat16 [32768, 4096], P('seq', 'head'), may hold values from -6 to 6
- out_weight: bfloat16 [32, 128, 4096], P('head'), may hold values from -0.09375 to 0.09375
Outputs:
- query_grad: bfloat16 [32768, 32, 128], P('seq', 'head')
- key_grad: bfloat16 [32768, 32, 128], P('seq', 'head')
- value_grad: bfloat16 [32768, 32, 128], P('seq', 'head')
All inputs are finite; a program needn't handle non-finite values.
Results may differ from a plain program's by a relative error of at most 0.0058.
Values may be sent and summed in bfloat16 or wider, within the bound.
No kernel may reach another device: no remote copies, remote signals or barrier semaphores. Data moves between devices by JAX's collectives and lax.ppermute only.
A program may use at most 128 MiB of HBM per device.

v0:
```python
import math
import jax
import jax.numpy as jnp
from jax import lax
from jax.sharding import PartitionSpec as P

BLOCK = 256


def body(queries, key_rows, value_rows, out_grad, out_weight):
    tokens = queries.shape[0]
    heads = queries.shape[1]
    depth = queries.shape[2]
    blocks = tokens // BLOCK
    factor = 1.0 / math.sqrt(depth * tokens * lax.axis_size("seq"))
    attn_grad = jnp.einsum(
        "tm,hdm->thd",
        lax.all_gather(out_grad, "head", axis=1, tiled=True),
        out_weight,
        preferred_element_type=jnp.float32,
    ).astype(jnp.bfloat16)
    layout = (blocks, BLOCK, heads, depth)
    query_blocks = queries.reshape(layout)
    key_blocks = key_rows.reshape(layout)
    value_blocks = value_rows.reshape(layout)
    grad_blocks = attn_grad.reshape(layout)
    kv_parts = jnp.einsum(
        "bthd,bthe->bhde", key_blocks, value_blocks, preferred_element_type=jnp.float32
    )
    qg_parts = jnp.einsum(
        "bthd,bthe->bhde", query_blocks, grad_blocks, preferred_element_type=jnp.float32
    )
    kv_total = jnp.sum(kv_parts, 0)
    qg_total = jnp.sum(qg_parts, 0)
    shards = lax.axis_size("seq")
    stacked = jnp.stack([kv_total, qg_total]).reshape(2, shards, -1)
    pieces = lax.all_to_all(stacked, "seq", split_axis=1, concat_axis=1, tiled=True)
    forward_sums = jnp.cumsum(pieces[0], 0) - pieces[0]
    reverse_sums = jnp.cumsum(pieces[1][::-1], 0)[::-1] - pieces[1]
    totals = lax.all_to_all(
        jnp.stack([forward_sums, reverse_sums]), "seq", split_axis=1, concat_axis=1, tiled=True
    )
    totals = totals.reshape(2, heads, depth, depth)
    before = totals[0]
    after = totals[1]
    first_zero = jnp.zeros((1, heads, depth, depth), jnp.float32)
    running = jnp.cumsum(kv_parts, 0)
    prefix = before[None] + jnp.concatenate([first_zero, running[:-1]], 0)
    backward_sums = jnp.cumsum(qg_parts[::-1], 0)[::-1]
    suffix = after[None] + jnp.concatenate([backward_sums[1:], first_zero], 0)
    prefix_bf = prefix.astype(jnp.bfloat16)
    suffix_bf = suffix.astype(jnp.bfloat16)
    causal = jnp.tril(jnp.ones((BLOCK, BLOCK), bool))
    qk_scores = jnp.einsum(
        "bthd,bshd->bhts", query_blocks, key_blocks, preferred_element_type=jnp.float32
    )
    qk_scores = jnp.where(causal, qk_scores, 0.0).astype(jnp.bfloat16)
    grad_scores = jnp.einsum(
        "bthd,bshd->bhts", grad_blocks, value_blocks, preferred_element_type=jnp.float32
    )
    grad_scores = jnp.where(causal, grad_scores, 0.0).astype(jnp.bfloat16)
    query_grad = jnp.einsum(
        "bhts,bshd->bthd", grad_scores, key_blocks, preferred_element_type=jnp.float32
    )
    query_grad = query_grad + jnp.einsum(
        "bthe,bhde->bthd", grad_blocks, prefix_bf, preferred_element_type=jnp.float32
    )
    key_grad = jnp.einsum(
        "bhts,bthd->bshd", grad_scores, query_blocks, preferred_element_type=jnp.float32
    )
    key_grad = key_grad + jnp.einsum(
        "bshe,bhde->bshd", value_blocks, suffix_bf, preferred_element_type=jnp.float32
    )
    value_grad = jnp.einsum(
        "bhts,bthe->bshe", qk_scores, grad_blocks, preferred_element_type=jnp.float32
    )
    value_grad = value_grad + jnp.einsum(
        "bshd,bhde->bshe", key_blocks, suffix_bf, preferred_element_type=jnp.float32
    )
    final_shape = (tokens, heads, depth)
    return (
        (factor * query_grad).astype(jnp.bfloat16).reshape(final_shape),
        (factor * key_grad).astype(jnp.bfloat16).reshape(final_shape),
        (factor * value_grad).astype(jnp.bfloat16).reshape(final_shape),
    )


def solution(mesh):
    placed = (
        P("seq", "head", None),
        P("seq", "head", None),
        P("seq", "head", None),
        P("seq", "head"),
        P("head", None, None),
    )
    return jax.shard_map(
        body,
        mesh=mesh,
        in_specs=placed,
        out_specs=(P("seq", "head", None), P("seq", "head", None), P("seq", "head", None)),
        check_vma=False,
    )
```

profile of v0, /device:TPU:32, one launch (start us, length us, event | category | flops | bytes accessed | tf_op | source)
XLA Modules:
  0.0 155.0 jit_solution(7390798430991049583)
XLA Ops:
  7.2 0.7 all-gather.2.cloned.1.call-update
  7.9 2.1 %fusion.38 = (f32[4,128,128]{2,1,0:T(8,128)S(1)}, f32[4,4,128,128]{3,2,1,0:T(8,128)S(1)}) fusion(bf16[4,256,4,128]{3,2,1,0:T(4,128)(2,1)} %bitcast.53, bf16[4,256,4,128]{3,2,1,0:T(4,128)(2,1)} %bitcast.46), kind=kOutput, calls=%fused_computation.48 | convolution fusion | flops 134414336 | bytes 3407872 | tf_op jit(solution)/shard_map/bthd,bthe->bhde/dot_general | solution.py:27
  10.0 54.7 %all-gather.2.cloned.1.call-done = bf16[1024,4096]{1,0:T(8,128)(2,1)} async-done(((bf16[1024,512]{1,0:T(8,128)(2,1)}), bf16[1024,4096]{1,0:T(8,128)(2,1)}) %all-gather.2.cloned.1.call-update) | async-done | bytes 8388624 | tf_op jit(solution)/shard_map/all_gather | solution.py:18
  64.7 8.2 %fusion.7 = bf16[1024,4,128]{2,0,1:T(8,128)(2,1)S(1)} fusion(bf16[4,128,4096]{2,1,0:T(8,128)(2,1)} %param.9, bf16[1024,4096]{1,0:T(8,128)(2,1)} %all-gather.2.cloned.1.call-done), kind=kOutput, calls=%fused_computation.12 | convolution fusion | flops 4295491584 | bytes 13631488 | tf_op jit(solution)/shard_map/tm,hdm->thd/dot_general | solution.py:16
  73.0 1.2 fusion.37
  74.2 1.1 copy.83
  75.4 1.2 copy.84
  76.6 10.1 %all-to-all-start = ((f32[2,32,2048]{2,0,1:T(2,128)}), f32[2,32,2048]{2,0,1:T(2,128)}, u32[]{:S(2)}, u32[]{:S(2)}) async-start(f32[2,32,2048]{2,0,1:T(2,128)} %copy.84), calls=%async_computation | async-start | bytes 1048576 | tf_op jit(solution)/shard_map/all_to_all | solution.py:37
  86.8 0.8 fusion.39
  87.6 1.0 copy-done.9
  88.6 0.8 fusion.40
  89.5 0.9 slice.31
  90.4 0.5 copy-done.5
  90.9 1.9 %select_convert_fusion.1 = bf16[4,4,256,256]{3,2,1,0:T(8,128)(2,1)S(1)} fusion(pred[256,256]{1,0:T(8,128)(4,1)S(1)} %iota_compare_fusion, bf16[4,256,4,128]{3,2,1,0:T(4,128)(2,1)S(1)} %bitcast.54, bf16[4,256,4,128]{3,1,0,2:T(8,128)(2,1)} %bitcast.57), kind=kOutput, calls=%fused_computation.3 | convolution fusion | flops 270532608 | bytes 4259840 | tf_op jit(solution)/shard_map/bthd,bshd->bhts/dot_general | solution.py:58
  92.9 12.0 %all-to-all-done = f32[2,32,2048]{2,0,1:T(2,128)} async-done(((f32[2,32,2048]{2,0,1:T(2,128)}), f32[2,32,2048]{2,0,1:T(2,128)}, u32[]{:S(2)}, u32[]{:S(2)}) %all-to-all-start) | async-done | bytes 524320 | tf_op jit(solution)/shard_map/all_to_all | solution.py:37
  104.9 1.7 %fusion.36 = (f32[1,32,2048]{2,0,1:T(1,128)S(1)}, f32[1,32,2048]{2,0,1:T(1,128)S(1)}) fusion(f32[2,32,2048]{2,0,1:T(2,128)} %all-to-all-done), kind=kLoop, calls=%fused_computation.46 | loop fusion | bytes 1048576 | tf_op jit(solution)/shard_map/slice | solution.py:38
  107.1 0.3 rev.10
  108.1 1.2 copy.87
  109.3 4.9 %all-to-all-start.1 = ((f32[2,32,2048]{2,0,1:T(2,128)}), f32[2,32,2048]{2,0,1:T(2,128)}, u32[]{:S(2)}, u32[]{:S(2)}) async-start(f32[2,32,2048]{2,0,1:T(2,128)} %copy.87), calls=%async_computation.1 | async-start | bytes 1048576 | tf_op jit(solution)/shard_map/all_to_all | solution.py:40
  114.2 3.4 %fusion.13 = f32[4,4,256,128]{3,2,1,0:T(8,128)} fusion(bf16[4,4,256,256]{3,2,1,0:T(8,128)(2,1)S(1)} %select_convert_fusion.1, bf16[4,256,4,128]{3,2,1,0:T(4,128)(2,1)} %bitcast.50), kind=kOutput, calls=%fused_computation.18 | convolution fusion | flops 268435456 | bytes 5242880 | tf_op jit(solution)/shard_map/bhts,bthd->bshd/dot_general | solution.py:68
  117.6 2.0 %fusion.24 = f32[4,4,256,128]{3,2,1,0:T(8,128)} fusion(bf16[4,4,256,256]{3,2,1,0:T(8,128)(2,1)S(1)} %select_convert_fusion.1, bf16[4,256,4,128]{3,2,1,0:T(4,128)(2,1)S(1)} %bitcast.47), kind=kOutput, calls=%fused_computation.28 | convolution fusion | flops 268435456 | bytes 5242880 | tf_op jit(solution)/shard_map/bhts,bshd->bthd/dot_general | solution.py:62
  119.7 3.9 %fusion.6 = f32[4,4,128,256]{3,2,1,0:T(8,128)} fusion(pred[256,256]{1,0:T(8,128)(4,1)S(1)} %iota_compare_fusion, bf16[4,256,4,128]{3,2,1,0:T(4,128)(2,1)} %bitcast.51, bf16[4,256,4,128]{3,2,1,0:T(4,128)(2,1)S(1)} %bitcast.48, bf16[4,256,4,128]{3,1,0,2:T(8,128)(2,1)} %bitcast.58), kind=kOutput, calls=%fused_computation.11 | convolution fusion | flops 538968064 | bytes 5308416 | tf_op jit(solution)/shard_map/bhts,bthe->bshe/dot_general | solution.py:74
  123.6 8.1 %all-to-all-done.1 = f32[2,32,2048]{2,0,1:T(2,128)} async-done(((f32[2,32,2048]{2,0,1:T(2,128)}), f32[2,32,2048]{2,0,1:T(2,128)}, u32[]{:S(2)}, u32[]{:S(2)}) %all-to-all-start.1) | async-done | bytes 524320 | tf_op jit(solution)/shard_map/all_to_all | solution.py:40
  131.7 2.5 %fusion.35 = (f32[1,32,2048]{2,0,1:T(1,128)S(1)}, f32[1,32,2048]{2,0,1:T(1,128)}) fusion(f32[2,32,2048]{2,0,1:T(2,128)} %all-to-all-done.1), kind=kLoop, calls=%fused_computation.45 | loop fusion | bytes 1048576 | tf_op jit(solution)/shard_map/slice | solution.py:45
  134.3 3.0 %fusion.10 = bf16[4,256,4,128]{1,3,2,0:T(8,128)(2,1)} fusion(f32[4,4,128,256]{3,2,1,0:T(8,128)} %fusion.6, bf16[4,256,4,128]{3,2,1,0:T(4,128)(2,1)S(1)} %bitcast.49, f32[3,4,128,128]{2,3,1,0:T(8,128)S(1)} %copy-done.3, f32[4,128,128]{1,2,0:T(8,128)S(1)} %copy.93), kind=kOutput, calls=%fused_computation.13 | convolution fusion | flops 136314880 | bytes 5242880 | tf_op jit(solution)/shard_map/bshd,bhde->bshe/dot_general | solution.py:77
  137.3 2.4 %copy.102 = bf16[4,256,4,128]{3,1,0,2:T(8,128)(2,1)} copy(bf16[4,256,4,128]{1,3,2,0:T(8,128)(2,1)} %fusion.10) | data formatting | bytes 2097152 | tf_op jit(solution)/shard_map/convert_element_type | solution.py:84
  139.7 3.1 %copy.105 = bf16[1024,4,128]{2,1,0:T(4,128)(2,1)} copy(bf16[1024,4,128]{2,0,1:T(8,128)(2,1)} %bitcast.60) | data formatting | bytes 2097152
  142.8 0.5 fusion.3
  143.5 1.8 %copy.104 = bf16[1024,4,128]{2,1,0:T(4,128)(2,1)} copy(bf16[1024,4,128]{2,0,1:T(8,128)(2,1)S(1)} %bitcast.61) | data formatting | bytes 2097152
  145.3 0.5 slice-done
  145.8 0.4 fusion.5
  146.4 1.8 %copy.103 = bf16[1024,4,128]{2,1,0:T(4,128)(2,1)} copy(bf16[1024,4,128]{2,0,1:T(8,128)(2,1)S(1)} %bitcast.62) | data formatting | bytes 2097152
  (39 shorter events, 1.9 us)
Async XLA Ops:
  7.2 57.6 %all-gather.2.cloned.1.call-start = ((), (), s32[]{:S(2)}) async-start(), calls=%async_computation.2 | async-start | bytes 9437184 | tf_op jit(solution)/shard_map/all_gather | solution.py:18
  10.0 62.9 %copy-start.4 = (bf16[1024,4,128]{2,1,0:T(4,128)(2,1)S(1)}, bf16[1024,4,128]{2,1,0:T(4,128)(2,1)}, u32[]{:S(2)}) copy-start(bf16[1024,4,128]{2,1,0:T(4,128)(2,1)} %param.5) | copy-start | bytes 3145732
  72.9 1.3 copy-start.7
  76.6 28.3 %all-to-all-start = ((f32[2,32,2048]{2,0,1:T(2,128)}), f32[2,32,2048]{2,0,1:T(2,128)}, u32[]{:S(2)}, u32[]{:S(2)}) async-start(f32[2,32,2048]{2,0,1:T(2,128)} %copy.84), calls=%async_computation | async-start | bytes 1048576 | tf_op jit(solution)/shard_map/all_to_all | solution.py:37
  87.5 1.0 copy-start.9
  89.4 1.5 copy-start.5
  109.3 22.4 %all-to-all-start.1 = ((f32[2,32,2048]{2,0,1:T(2,128)}), f32[2,32,2048]{2,0,1:T(2,128)}, u32[]{:S(2)}, u32[]{:S(2)}) async-start(f32[2,32,2048]{2,0,1:T(2,128)} %copy.87), calls=%async_computation.1 | async-start | bytes 1048576 | tf_op jit(solution)/shard_map/all_to_all | solution.py:40
  114.2 3.4 %copy-start = (bf16[1024,4,128]{2,1,0:T(4,128)(2,1)S(1)}, bf16[1024,4,128]{2,1,0:T(4,128)(2,1)}, u32[]{:S(2)}) copy-start(bf16[1024,4,128]{2,1,0:T(4,128)(2,1)} %param.6) | copy-start | bytes 3145732
  123.6 10.7 %copy-start.3 = (f32[3,4,128,128]{2,3,1,0:T(8,128)S(1)}, f32[3,4,128,128]{2,3,1,0:T(8,128)}, u32[]{:S(2)}) copy-start(f32[3,4,128,128]{2,3,1,0:T(8,128)} %slice.31) | copy-start | bytes 2359300
  137.3 5.5 %copy-start.2 = (f32[4,4,256,128]{3,2,1,0:T(8,128)S(1)}, f32[4,4,256,128]{3,2,1,0:T(8,128)}, u32[]{:S(2)}) copy-start(f32[4,4,256,128]{3,2,1,0:T(8,128)} %fusion.13) | copy-start | bytes 6291460
  139.7 3.1 %copy-start.6 = (bf16[1024,4,128]{2,1,0:T(4,128)(2,1)S(1)}, bf16[1024,4,128]{2,1,0:T(4,128)(2,1)}, u32[]{:S(2)}) copy-start(bf16[1024,4,128]{2,1,0:T(4,128)(2,1)} %param.7) | copy-start | bytes 3145732
  143.3 1.9 %copy-start.1 = (f32[4,4,256,128]{3,2,1,0:T(8,128)S(1)}, f32[4,4,256,128]{3,2,1,0:T(8,128)}, u32[]{:S(2)}) copy-start(f32[4,4,256,128]{3,2,1,0:T(8,128)} %fusion.24) | copy-start | bytes 6291460
  143.3 1.9 %copy-start.8 = (bf16[1024,4,128]{2,0,1:T(8,128)(2,1)S(1)}, bf16[1024,4,128]{2,0,1:T(8,128)(2,1)}, u32[]{:S(2)}) copy-start(bf16[1024,4,128]{2,0,1:T(8,128)(2,1)} %copy-done.7) | copy-start | bytes 3145732
  143.3 2.4 %slice-start = ((f32[4,4,128,128]{3,2,1,0:T(8,128)}), f32[3,4,128,128]{3,2,1,0:T(8,128)S(1)}, s32[]{:S(2)}) async-start(f32[4,4,128,128]{3,2,1,0:T(8,128)} %copy-done.9), calls=%async_computation.3 | async-start | bytes 1572864 | tf_op jit(solution)/shard_map/slice | solution.py:48
  143.4 2.5 %copy-start.10 = (f32[1,32,2048]{2,0,1:T(1,128)S(1)}, f32[1,32,2048]{2,0,1:T(1,128)}, u32[]{:S(2)}) copy-start(f32[1,32,2048]{2,0,1:T(1,128)} %get-tuple-element.13) | copy-start | bytes 786436
Sparse Core Ops, SparseCore 0:
  9.8 54.8 all-gather.1
where the time goes:
time: 156 us; the launch traced here: 155 us
  waiting for transfers between devices  75.5 us (48%)
  matrix products  26.8 us (17%)
  local copies, waits for them, and re-layouts  21.1 us (14%)
  starting transfers between devices  15.1 us (10%)
  between operations  14.3 us (9%)
  other arithmetic  2.3 us (1%)
    all_gather x1, waiting for transfers between devices, body(): lax.all_gather(out_grad, 'head', axis=1, tiled=True)  54.7 us
    all_to_all x1, waiting for transfers between devices, body(): lax.all_to_all(stacked, 'seq', split_axis=1, concat_axis=1, tiled=True)  12 us
    all_to_all x1, starting transfers between devices, body(): lax.all_to_all(stacked, 'seq', split_axis=1, concat_axis=1, tiled=True)  10.1 us
    unnamed x27, local copies, waits for them, and re-layouts  8.39 us
    dot_general x1, matrix products, body(): jnp.einsum('tm,hdm->thd', lax.all_gather(out_grad, 'head', axis=1, tiled=...  8.22 us
    all_to_all x1, waiting for transfers between devices, body(): lax.all_to_all(jnp.stack([forward_sums, reverse_sums]), 'seq', split_axis...  8.12 us
    all_to_all x1, starting transfers between devices, body(): lax.all_to_all(jnp.stack([forward_sums, reverse_sums]), 'seq', split_axis...  4.9 us
    dot_general x1, matrix products, body(): jnp.einsum('bhts,bthe->bshe', qk_scores, grad_blocks, preferred_element_t...  3.89 us
  transfers between devices with their start and end apart: 3, of which 3 were waited for; matrix products, arithmetic and copies ran while one was open for 10% of the time, Pallas kernels for 0%

commit v1 on v0

--- a/solution.py
+++ b/solution.py
@@ -15,7 +15,10 @@
     factor = 1.0 / math.sqrt(depth * tokens * lax.axis_size("seq"))
     attn_grad = jnp.einsum(
         "tm,hdm->thd",
-        lax.all_gather(out_grad, "head", axis=1, tiled=True),
+        jnp.concatenate(
+            lax.all_to_all(jnp.stack(lax.axis_size("head") * [out_grad], axis=0), "head", 0, 0),
+            axis=1,
+        ),
         out_weight,
         preferred_element_type=jnp.float32,
     ).astype(jnp.bfloat16)

time: 156 us -> 243 us (1.56)
  local copies, waits for them, and re-layouts: 21.1 us -> 69.4 us
  waiting for transfers between devices: 75.5 us -> 113 us
  between operations: 14.3 us -> 0.89 us
  other arithmetic: 2.3 us -> 10.2 us
  starting transfers between devices: 15.1 us -> 21.4 us
    all_to_all x0 -> x1, waiting for transfers between devices: none -> 93.3 us  [body(): lax.all_to_all(jnp.stack(lax.axis_size('head') * [out_grad], axis=0), 'he...]
    all_gather x1 -> x0, waiting for transfers between devices: 54.7 us -> none  [body(): lax.all_gather(out_grad, 'head', axis=1, tiled=True)]
    reshape x0 -> x2, local copies, waits for them, and re-layouts: none -> 24.8 us  [body(): jnp.concatenate(lax.all_to_all(jnp.stack(lax.axis_size('head') * [out_gra...]
    rev x2, local copies, waits for them, and re-layouts: 0.59 us -> 15.9 us  [body(): reverse_sums = jnp.cumsum(pieces[1][::-1], 0)[::-1] - pieces[1]]
    another operation x0 -> x1, local copies, waits for them, and re-layouts: none -> 5.17 us  [body(): jnp.stack(lax.axis_size('head') * [out_grad], axis=0)]
    all_to_all x0 -> x1, starting transfers between devices: none -> 5.07 us  [body(): lax.all_to_all(jnp.stack(lax.axis_size('head') * [out_grad], axis=0), 'he...]
    unnamed x27 -> x31, local copies, waits for them, and re-layouts: 8.39 us -> 9.97 us
  transfers between devices with their start and end apart: 3 -> 3, of which waited for: 3 -> 3; matrix products, arithmetic and copies ran while one was open for 10% -> 6% of each run, Pallas kernels for 0% -> 0%
where the time goes in v1:
time: 243 us; the launch traced here: 240 us
  waiting for transfers between devices  113 us (47%)
  local copies, waits for them, and re-layouts  69.4 us (29%)
  matrix products  25.5 us (10%)
  starting transfers between devices  21.4 us (9%)
  other arithmetic  10.2 us (4%)
    all_to_all x1, waiting for transfers between devices, body(): lax.all_to_all(jnp.stack(lax.axis_size('head') * [out_grad], axis=0), 'he...  93.3 us
    reshape x2, local copies, waits for them, and re-layouts, body(): jnp.concatenate(lax.all_to_all(jnp.stack(lax.axis_size('head') * [out_gra...  24.8 us
    rev x2, local copies, waits for them, and re-layouts, body(): reverse_sums = jnp.cumsum(pieces[1][::-1], 0)[::-1] - pieces[1]  15.9 us
    all_to_all x1, waiting for transfers between devices, body(): lax.all_to_all(stacked, 'seq', split_axis=1, concat_axis=1, tiled=True)  11.6 us
    all_to_all x1, starting transfers between devices, body(): lax.all_to_all(stacked, 'seq', split_axis=1, concat_axis=1, tiled=True)  11.4 us
    unnamed x31, local copies, waits for them, and re-layouts  9.97 us
    dot_general x1, matrix products, body(): jnp.einsum('tm,hdm->thd', jnp.concatenate(lax.all_to_all(jnp.stack(lax.ax...  8.29 us
    all_to_all x1, waiting for transfers between devices, body(): lax.all_to_all(jnp.stack([forward_sums, reverse_sums]), 'seq', split_axis...  7.76 us
  transfers between devices with their start and end apart: 3, of which 3 were waited for; matrix products, arithmetic and copies ran while one was open for 6% of the time, Pallas kernels for 0%

profile of v1, /device:TPU:32, one launch (start us, length us, event | category | flops | bytes accessed | tf_op | source)
XLA Modules:
  0.0 240.0 jit_solution(6791500627112123716)
XLA Ops:
  0.6 5.2 %stack.12 = bf16[8,1024,512]{2,1,0:T(8,128)(2,1)} broadcast(bf16[1024,512]{1,0:T(8,128)(2,1)} %param.8), dimensions={1,2} | broadcast | bytes 9437184 | tf_op jit(solution)/shard_map/stack | solution.py:19
  5.8 5.1 %all-to-all-start = ((bf16[8,1024,512]{2,1,0:T(8,128)(2,1)}), bf16[8,1024,512]{2,1,0:T(8,128)(2,1)}, u32[]{:S(2)}, u32[]{:S(2)}) async-start(bf16[8,1024,512]{2,1,0:T(8,128)(2,1)} %stack.12), calls=%async_computation | async-start | bytes 16777216 | tf_op jit(solution)/shard_map/all_to_all | solution.py:19
  12.2 93.3 %all-to-all-done = bf16[8,1024,512]{2,1,0:T(8,128)(2,1)} async-done(((bf16[8,1024,512]{2,1,0:T(8,128)(2,1)}), bf16[8,1024,512]{2,1,0:T(8,128)(2,1)}, u32[]{:S(2)}, u32[]{:S(2)}) %all-to-all-start) | async-done | bytes 8388640 | tf_op jit(solution)/shard_map/all_to_all | solution.py:19
  105.5 11.3 %copy.77 = bf16[1024,8,512]{2,1,0:T(8,128)(2,1)} copy(bf16[1024,8,512]{2,0,1:T(8,128)(2,1)} %bitcast) | data formatting | bytes 16777216 | tf_op jit(solution)/shard_map/reshape | solution.py:18
  116.8 13.5 %reshape.57 = bf16[1024,4096,1]{1,0,2:T(8,128)(2,1)} reshape(bf16[1024,8,512]{2,1,0:T(8,128)(2,1)} %copy.77) | data formatting | bytes 16777216 | tf_op jit(solution)/shard_map/reshape | solution.py:18
  130.3 8.3 %convolution_convert_fusion = bf16[1024,4,128]{2,0,1:T(8,128)(2,1)S(1)} fusion(bf16[1024,4096,1]{1,0,2:T(8,128)(2,1)} %reshape.57, bf16[4,128,4096]{2,1,0:T(8,128)(2,1)} %param.9), kind=kOutput, calls=%fused_computation.10 | convolution fusion | flops 4295491584 | bytes 13631488 | tf_op jit(solution)/shard_map/tm,hdm->thd/dot_general | solution.py:16
  138.6 1.2 fusion.32
  139.9 1.1 copy.85
  141.7 1.1 pad_maximum_fusion
  142.8 1.2 copy.86
  144.0 11.4 %all-to-all-start.1 = ((f32[2,32,2048]{2,0,1:T(2,128)}), f32[2,32,2048]{2,0,1:T(2,128)}, u32[]{:S(2)}, u32[]{:S(2)}) async-start(f32[2,32,2048]{2,0,1:T(2,128)} %copy.86), calls=%async_computation.1 | async-start | bytes 1048576 | tf_op jit(solution)/shard_map/all_to_all | solution.py:40
  159.0 2.3 select_convert_fusion.1
  161.3 11.6 %all-to-all-done.1 = f32[2,32,2048]{2,0,1:T(2,128)} async-done(((f32[2,32,2048]{2,0,1:T(2,128)}), f32[2,32,2048]{2,0,1:T(2,128)}, u32[]{:S(2)}, u32[]{:S(2)}) %all-to-all-start.1) | async-done | bytes 524320 | tf_op jit(solution)/shard_map/all_to_all | solution.py:40
  172.9 1.7 fusion.31
  176.1 1.9 reduce_window_sum.34
  178.0 1.8 copy_subtract_fusion
  180.6 7.9 %rev.10 = f32[32,2048]{1,0:T(8,128)} reverse(f32[32,2048]{1,0:T(8,128)} %bitcast.61), dimensions={0} | reverse | bytes 524288 | tf_op jit(solution)/shard_map/rev | solution.py:42
  188.5 1.9 reduce_window_sum.35
  190.4 7.9 %rev.11 = f32[32,2048]{1,0:T(8,128)} reverse(f32[32,2048]{1,0:T(8,128)} %reduce_window_sum.35), dimensions={0} | reverse | bytes 524288 | tf_op jit(solution)/shard_map/rev | solution.py:42
  198.3 1.0 subtract_bitcast_fusion
  200.4 1.2 copy.89
  201.6 4.9 %all-to-all-start.2 = ((f32[2,32,2048]{2,0,1:T(2,128)}), f32[2,32,2048]{2,0,1:T(2,128)}, u32[]{:S(2)}, u32[]{:S(2)}) async-start(f32[2,32,2048]{2,0,1:T(2,128)} %copy.89), calls=%async_computation.2 | async-start | bytes 1048576 | tf_op jit(solution)/shard_map/all_to_all | solution.py:43
  206.5 3.3 %fusion.8 = f32[4,4,256,128]{3,2,1,0:T(8,128)} fusion(bf16[4,4,256,256]{3,2,1,0:T(8,128)(2,1)S(1)} %select_convert_fusion.1, bf16[4,256,4,128]{3,2,1,0:T(4,128)(2,1)} %bitcast.47), kind=kOutput, calls=%fused_computation.16 | convolution fusion | flops 268435456 | bytes 5242880 | tf_op jit(solution)/shard_map/bhts,bthd->bshd/dot_general | solution.py:71
  209.8 2.0 fusion.19
  211.8 3.9 %fusion.4 = f32[4,4,128,256]{3,2,1,0:T(8,128)} fusion(pred[256,256]{1,0:T(8,128)(4,1)S(1)} %iota_compare_fusion, bf16[4,256,4,128]{3,2,1,0:T(4,128)(2,1)} %bitcast.48, bf16[4,256,4,128]{3,2,1,0:T(4,128)(2,1)S(1)} %bitcast.45, bf16[4,256,4,128]{3,1,0,2:T(8,128)(2,1)} %bitcast.55), kind=kOutput, calls=%fused_computation.9 | convolution fusion | flops 538968064 | bytes 5308416 | tf_op jit(solution)/shard_map/bhts,bthe->bshe/dot_general | solution.py:77
  215.7 7.8 %all-to-all-done.2 = f32[2,32,2048]{2,0,1:T(2,128)} async-done(((f32[2,32,2048]{2,0,1:T(2,128)}), f32[2,32,2048]{2,0,1:T(2,128)}, u32[]{:S(2)}, u32[]{:S(2)}) %all-to-all-start.2) | async-done | bytes 524320 | tf_op jit(solution)/shard_map/all_to_all | solution.py:43
  223.5 2.5 %fusion.30 = (f32[1,32,2048]{2,0,1:T(1,128)S(1)}, f32[1,32,2048]{2,0,1:T(1,128)}) fusion(f32[2,32,2048]{2,0,1:T(2,128)} %all-to-all-done.2), kind=kLoop, calls=%fused_computation.43 | loop fusion | bytes 1048576 | tf_op jit(solution)/shard_map/slice | solution.py:48
  226.1 3.0 %fusion.5 = bf16[4,256,4,128]{1,3,2,0:T(8,128)(2,1)} fusion(f32[4,4,128,256]{3,2,1,0:T(8,128)} %fusion.4, bf16[4,256,4,128]{3,2,1,0:T(4,128)(2,1)S(1)} %bitcast.46, f32[3,4,128,128]{2,3,1,0:T(8,128)S(1)} %copy-done.3, f32[4,128,128]{1,2,0:T(8,128)S(1)} %copy.95), kind=kOutput, calls=%fused_computation.11 | convolution fusion | flops 136314880 | bytes 5242880 | tf_op jit(solution)/shard_map/bshd,bhde->bshe/dot_general | solution.py:80
  229.1 2.4 %copy.104 = bf16[4,256,4,128]{3,1,0,2:T(8,128)(2,1)} copy(bf16[4,256,4,128]{1,3,2,0:T(8,128)(2,1)} %fusion.5) | data formatting | bytes 2097152 | tf_op jit(solution)/shard_map/convert_element_type | solution.py:87
  231.6 3.1 %copy.107 = bf16[1024,4,128]{2,1,0:T(4,128)(2,1)} copy(bf16[1024,4,128]{2,0,1:T(8,128)(2,1)} %bitcast.57) | data formatting | bytes 2097152
  235.3 1.8 copy.106
  238.2 1.8 copy.105
  (45 shorter events, 10.8 us)
Async XLA Ops:
  5.8 5.1 %copy-start = (bf16[1024,4,128]{2,1,0:T(4,128)(2,1)S(1)}, bf16[1024,4,128]{2,1,0:T(4,128)(2,1)}, u32[]{:S(2)}) copy-start(bf16[1024,4,128]{2,1,0:T(4,128)(2,1)} %param.6) | copy-start | bytes 3145732
  5.8 5.1 %copy-start.6 = (bf16[1024,4,128]{2,1,0:T(4,128)(2,1)S(1)}, bf16[1024,4,128]{2,1,0:T(4,128)(2,1)}, u32[]{:S(2)}) copy-start(bf16[1024,4,128]{2,1,0:T(4,128)(2,1)} %param.7) | copy-start | bytes 3145732
  5.8 99.7 %all-to-all-start = ((bf16[8,1024,512]{2,1,0:T(8,128)(2,1)}), bf16[8,1024,512]{2,1,0:T(8,128)(2,1)}, u32[]{:S(2)}, u32[]{:S(2)}) async-start(bf16[8,1024,512]{2,1,0:T(8,128)(2,1)} %stack.12), calls=%async_computation | async-start | bytes 16777216 | tf_op jit(solution)/shard_map/all_to_all | solution.py:19
  130.3 8.3 %copy-start.5 = (bf16[1024,4,128]{2,1,0:T(4,128)(2,1)S(1)}, bf16[1024,4,128]{2,1,0:T(4,128)(2,1)}, u32[]{:S(2)}) copy-start(bf16[1024,4,128]{2,1,0:T(4,128)(2,1)} %param.5) | copy-start | bytes 3145732
  138.6 1.2 copy-start.8
  144.0 28.9 %all-to-all-start.1 = ((f32[2,32,2048]{2,0,1:T(2,128)}), f32[2,32,2048]{2,0,1:T(2,128)}, u32[]{:S(2)}, u32[]{:S(2)}) async-start(f32[2,32,2048]{2,0,1:T(2,128)} %copy.86), calls=%async_computation.1 | async-start | bytes 1048576 | tf_op jit(solution)/shard_map/all_to_all | solution.py:40
  156.2 1.0 copy-start.10
  174.6 0.7 copy-start.11
  201.6 21.9 %all-to-all-start.2 = ((f32[2,32,2048]{2,0,1:T(2,128)}), f32[2,32,2048]{2,0,1:T(2,128)}, u32[]{:S(2)}, u32[]{:S(2)}) async-start(f32[2,32,2048]{2,0,1:T(2,128)} %copy.89), calls=%async_computation.2 | async-start | bytes 1048576 | tf_op jit(solution)/shard_map/all_to_all | solution.py:43
  215.7 10.4 %copy-start.3 = (f32[3,4,128,128]{2,3,1,0:T(8,128)S(1)}, f32[3,4,128,128]{2,3,1,0:T(8,128)}, u32[]{:S(2)}) copy-start(f32[3,4,128,128]{2,3,1,0:T(8,128)} %slice.31) | copy-start | bytes 2359300
  229.1 5.5 %copy-start.2 = (f32[4,4,256,128]{3,2,1,0:T(8,128)S(1)}, f32[4,4,256,128]{3,2,1,0:T(8,128)}, u32[]{:S(2)}) copy-start(f32[4,4,256,128]{3,2,1,0:T(8,128)} %fusion.8) | copy-start | bytes 6291460
  229.1 5.5 %copy-start.4 = (f32[3,4,128,128]{2,3,1,0:T(8,128)S(1)}, f32[3,4,128,128]{2,3,1,0:T(8,128)}, u32[]{:S(2)}) copy-start(f32[3,4,128,128]{2,3,1,0:T(8,128)} %slice.31) | copy-start | bytes 2359300
  231.6 3.1 %copy-start.7 = (bf16[1024,4,128]{2,1,0:T(4,128)(2,1)S(1)}, bf16[1024,4,128]{2,1,0:T(4,128)(2,1)}, u32[]{:S(2)}) copy-start(bf16[1024,4,128]{2,1,0:T(4,128)(2,1)} %param.7) | copy-start | bytes 3145732
  235.2 1.9 copy-start.1
  235.2 1.9 copy-start.9
  235.2 2.4 %slice-start = ((f32[4,4,128,128]{3,2,1,0:T(8,128)}), f32[3,4,128,128]{3,2,1,0:T(8,128)S(1)}, s32[]{:S(2)}) async-start(f32[4,4,128,128]{3,2,1,0:T(8,128)} %copy-done.10), calls=%async_computation.3 | async-start | bytes 1572864 | tf_op jit(solution)/shard_map/slice | solution.py:51
  235.2 2.5 %copy-start.12 = (f32[1,32,2048]{2,0,1:T(1,128)S(1)}, f32[1,32,2048]{2,0,1:T(1,128)}, u32[]{:S(2)}) copy-start(f32[1,32,2048]{2,0,1:T(1,128)} %get-tuple-element.13) | copy-start | bytes 786436
